TPU v7x, 32 devices: a whole 2x2x4 slice. The times are simulated.
32 devices in a mesh: parts: 2 (over y), layer: 2 (over core), row: 2 (over x), col: 4 (over z).
Axes of the slice: x: 2, y: 2, z: 4, core: 2. Of those that a mesh axis runs over, the one named last changes fastest.
Arguments:
- density_blocks: bfloat16 [192, 256, 64], P(('parts', 'layer', 'row'), 'col'), parts along dimension 0, may hold values from -0.5 to 0.5
- left_index: int32 [192, 16, 8], P(('parts', 'row'), 'col'), parts along dimension 0, may hold values from 0 to 23
- right_index: int32 [192, 16, 8], P(('parts', 'row'), 'col'), parts along dimension 0, may hold values from 0 to 23
- pair_count: int32 [192, 16], P(('parts', 'row'), 'col'), parts along dimension 0, may hold values from 1 to 8, as said below
Outputs:
- square: bfloat16 [192, 256, 64], P(('parts', 'layer', 'row'), 'col'), parts along dimension 0
There are 2 independent parts, one for each index of `parts`. A program takes and returns all parts, laid end to end along the dimension named above; each array names one. Nothing has to cross between parts.
Inputs may be any that keep to these rules, and one draw needn't show every extreme that they name: `pair_count`: every result panel has at least one result block and inner panel with 8 live pairs; the same pair may be listed twice and then counts twice.
All inputs are finite; a program needn't handle non-finite values.
Results may differ from a plain program's by a relative error of at most 0.001.
Values may be sent and summed in bfloat16 or wider, within the bound.
A program may use at most 64 MiB of HBM per device.

v0:
```python
import jax
import jax.numpy as jnp
from jax import lax
from jax.sharding import PartitionSpec as P


def passed_along(shard, axis, by):
    devices = lax.axis_size(axis)
    return lax.ppermute(shard, axis, [(i, (i + by) % devices) for i in range(devices)])


def block_terms(left_panel, right_panel, left_pick, right_pick, counts):
    live_mask = lax.broadcasted_iota(jnp.int32, left_pick.shape, 1) < counts[:, None]
    picked_left = jnp.take(left_panel, left_pick, axis=0)
    picked_right = jnp.take(right_panel, right_pick, axis=0)
    picked_right = jnp.where(
        live_mask[:, :, None, None], picked_right, jnp.zeros((), picked_right.dtype)
    )
    return jnp.einsum(
        "rpij,rpjl->ril", picked_left, picked_right, preferred_element_type=jnp.float32
    )


def panel_terms(left_panel, right_panel, left_pick, right_pick, counts):
    return block_terms(left_panel, right_panel, left_pick, right_pick, counts)


def inner_slice(values, inner_panel):
    return lax.dynamic_index_in_dim(values, inner_panel, 1, keepdims=False)


def on_device(density_blocks, left_index, right_index, pair_count):
    slot_count = density_blocks.shape[0]
    columns = lax.axis_size("col")
    layer_at = lax.axis_index("layer")
    column_at = lax.axis_index("col")
    own_left = lax.dynamic_slice_in_dim(left_index, layer_at * slot_count, slot_count, 0)
    own_right = lax.dynamic_slice_in_dim(right_index, layer_at * slot_count, slot_count, 0)
    own_count = lax.dynamic_slice_in_dim(pair_count, layer_at * slot_count, slot_count, 0)
    column_panels = lax.all_gather(density_blocks, ("layer", "row"), axis=0, tiled=True)

    def flat_terms(held_panel, inner_panel):
        right_panel = lax.dynamic_slice_in_dim(
            column_panels, inner_panel * slot_count, slot_count, 0
        )
        return panel_terms(
            held_panel,
            right_panel,
            inner_slice(own_left, inner_panel),
            inner_slice(own_right, inner_panel),
            inner_slice(own_count, inner_panel),
        )

    def flat_step(offset, loop_state):
        held_panel, running = loop_state
        running = running + flat_terms(held_panel, (column_at + offset) % columns)
        held_panel = passed_along(held_panel, "col", -1)
        return (held_panel, running)

    initial = (density_blocks, jnp.zeros(density_blocks.shape, jnp.float32))
    held_panel, running = lax.fori_loop(0, columns - 1, flat_step, initial)
    running = running + flat_terms(held_panel, (column_at + columns - 1) % columns)
    return running.astype(jnp.bfloat16)


def solution(mesh):
    placed = (
        P(("parts", "layer", "row"), "col", None),
        P(("parts", "row"), "col", None),
        P(("parts", "row"), "col", None),
        P(("parts", "row"), "col"),
    )
    return jax.shard_map(
        on_device,
        mesh=mesh,
        in_specs=placed,
        out_specs=P(("parts", "layer", "row"), "col", None),
        check_vma=False,
    )
```

profile of v0, /device:TPU:0, one launch (start us, length us, event | category | flops | bytes accessed | tf_op | source)
XLA Modules:
  0.0 82.6 jit_solution(2040288365737321233)
XLA Ops:
  0.0 1.0 %copy.47 = bf16[24,64,64]{2,1,0:T(8,128)(2,1)S(1)} copy(bf16[24,64,64]{2,1,0:T(8,128)(2,1)} %param.8) | data formatting | bytes 393216
  1.0 0.8 constant_dynamic-slice_fusion.5
  1.9 29.6 %all_gather.3 = bf16[96,64,64]{2,1,0:T(8,128)(2,1)S(1)} all-gather(bf16[24,64,64]{2,1,0:T(8,128)(2,1)S(1)} %copy.47), channel_id=1, replica_groups=mesh['parts'=2,'layer'=2,'row'=2,'col'=4] {'layer','row'}, dimensions={0}, use_global_device_ids=true | all-gather | bytes 983040 | tf_op jit(solution)/shard_map/all_gather | solution.py:40
  31.5 39.6 %while.18 = (s32[]{:T(128)}, bf16[24,64,64]{2,1,0:T(8,128)(2,1)S(1)}, f32[24,64,64]{2,1,0:T(8,128)}, s32[]{:T(128)}, s32[24,4,8]{0,2,1:T(8,128)S(1)}, /*index=5*...) while((s32[]{:T(128)}, ...), condition=%wide.region_1.3_spmd.clone, body=%wide.region_0.2_spmd.clone.sunk | while | flops 103224920 | bytes 11823404 | solution.py:61
  31.5 4.5 %collective-permute-start = (bf16[24,64,64]{2,1,0:T(8,128)(2,1)S(1)}, bf16[24,64,64]{2,1,0:T(8,128)(2,1)S(1)}, u32[]{:S(2)}, u32[]{:S(2)}) collective-permute-start(bf16[24,64,64]{2,1,0:T(8,128)(2,1)S(1)} %copy.41), channel_id=1, source_target_pairs={{0,3},{1,0},{2,1},{3,2},{4,7},{5,4},{6,5},{7,6},{8,11},{9,8},{10,9... | collective-permute-start | bytes 589832 | tf_op jit(solution)/shard_map/while/body/eval_jaxpr/ppermute | solution.py:9
  36.0 0.1 copy.35
  36.2 0.1 reshape.118
  36.4 0.1 reshape.119
  36.5 2.7 %gather_fusion.1 = bf16[192,64,64]{2,1,0:T(8,128)(2,1)} fusion(bf16[24,64,64]{2,1,0:T(8,128)(2,1)S(1)} %copy.41, s32[1024]{0:T(1024)S(1)} %pad_clamp_fusion.7), kind=kCustom, calls=%fused_computation.clone.clone.1 | custom fusion | bytes 3146496 | tf_op jit(solution)/shard_map/while/body/eval_jaxpr/jit(_take)/gather | solution.py:14
  39.2 2.7 %gather_fusion = bf16[192,64,64]{2,1,0:T(8,128)(2,1)} fusion(bf16[24,64,64]{2,1,0:T(8,128)(2,1)S(1)} %constant_dynamic-slice_fusion.10, s32[1024]{0:T(1024)S(1)} %pad_clamp_fusion.6), kind=kCustom, calls=%fused_computation.1.clone.clone.1 | custom fusion | bytes 3146496 | tf_op jit(solution)/shard_map/while/body/eval_jaxpr/jit(_take)/gather | solution.py:15
  42.0 4.7 %fusion.39 = f32[24,64,64]{2,1,0:T(8,128)} fusion(bf16[24,8,64,64]{3,2,1,0:T(8,128)(2,1)} %bitcast.51, pred[24,8]{1,0:T(8,128)(4,1)S(1)} %compare_and_fusion.6, pred[24,8]{1,0:T(8,128)(4,1)S(1)} %iota_compare_fusion.3, bf16[24,8,64,64]{3,2,1,0:T(8,128)(2,1)} %bitcast.50, pred[24,8]{1,0:T(8,128)(4,1)S(1)} %compare_and_fusion.7, ...), kind=kOutput, calls=%fused_computation.13.clone.1 | convolution fusion | flops 103219200 | bytes 3932737 | tf_op jit(solution)/shard_map/while/body/eval_jaxpr/rpij,rpjl->ril/dot_general | solution.py:19
  46.7 1.8 %collective-permute-start = (bf16[24,64,64]{2,1,0:T(8,128)(2,1)S(1)}, bf16[24,64,64]{2,1,0:T(8,128)(2,1)S(1)}, u32[]{:S(2)}, u32[]{:S(2)}) collective-permute-start(bf16[24,64,64]{2,1,0:T(8,128)(2,1)S(1)} %copy.41), channel_id=1, source_target_pairs={{0,3},{1,0},{2,1},{3,2},{4,7},{5,4},{6,5},{7,6},{8,11},{9,8},{10,9... | collective-permute-start | bytes 589832 | tf_op jit(solution)/shard_map/while/body/eval_jaxpr/ppermute | solution.py:9
  48.5 0.1 copy.35
  48.7 0.1 reshape.118
  48.9 0.1 reshape.119
  49.0 2.7 %gather_fusion.1 = bf16[192,64,64]{2,1,0:T(8,128)(2,1)} fusion(bf16[24,64,64]{2,1,0:T(8,128)(2,1)S(1)} %copy.41, s32[1024]{0:T(1024)S(1)} %pad_clamp_fusion.7), kind=kCustom, calls=%fused_computation.clone.clone.1 | custom fusion | bytes 3146496 | tf_op jit(solution)/shard_map/while/body/eval_jaxpr/jit(_take)/gather | solution.py:14
  51.8 2.7 %gather_fusion = bf16[192,64,64]{2,1,0:T(8,128)(2,1)} fusion(bf16[24,64,64]{2,1,0:T(8,128)(2,1)S(1)} %constant_dynamic-slice_fusion.10, s32[1024]{0:T(1024)S(1)} %pad_clamp_fusion.6), kind=kCustom, calls=%fused_computation.1.clone.clone.1 | custom fusion | bytes 3146496 | tf_op jit(solution)/shard_map/while/body/eval_jaxpr/jit(_take)/gather | solution.py:15
  54.5 4.9 %fusion.39 = f32[24,64,64]{2,1,0:T(8,128)} fusion(bf16[24,8,64,64]{3,2,1,0:T(8,128)(2,1)} %bitcast.51, pred[24,8]{1,0:T(8,128)(4,1)S(1)} %compare_and_fusion.6, pred[24,8]{1,0:T(8,128)(4,1)S(1)} %iota_compare_fusion.3, bf16[24,8,64,64]{3,2,1,0:T(8,128)(2,1)} %bitcast.50, pred[24,8]{1,0:T(8,128)(4,1)S(1)} %compare_and_fusion.7, ...), kind=kOutput, calls=%fused_computation.13.clone.1 | convolution fusion | flops 103219200 | bytes 3932737 | tf_op jit(solution)/shard_map/while/body/eval_jaxpr/rpij,rpjl->ril/dot_general | solution.py:19
  59.5 0.7 collective-permute-start
  60.4 0.1 reshape.118
  60.5 0.1 reshape.119
  60.6 2.7 %gather_fusion.1 = bf16[192,64,64]{2,1,0:T(8,128)(2,1)} fusion(bf16[24,64,64]{2,1,0:T(8,128)(2,1)S(1)} %copy.41, s32[1024]{0:T(1024)S(1)} %pad_clamp_fusion.7), kind=kCustom, calls=%fused_computation.clone.clone.1 | custom fusion | bytes 3146496 | tf_op jit(solution)/shard_map/while/body/eval_jaxpr/jit(_take)/gather | solution.py:14
  63.4 2.7 %gather_fusion = bf16[192,64,64]{2,1,0:T(8,128)(2,1)} fusion(bf16[24,64,64]{2,1,0:T(8,128)(2,1)S(1)} %constant_dynamic-slice_fusion.10, s32[1024]{0:T(1024)S(1)} %pad_clamp_fusion.6), kind=kCustom, calls=%fused_computation.1.clone.clone.1 | custom fusion | bytes 3146496 | tf_op jit(solution)/shard_map/while/body/eval_jaxpr/jit(_take)/gather | solution.py:15
  66.1 4.9 %fusion.39 = f32[24,64,64]{2,1,0:T(8,128)} fusion(bf16[24,8,64,64]{3,2,1,0:T(8,128)(2,1)} %bitcast.51, pred[24,8]{1,0:T(8,128)(4,1)S(1)} %compare_and_fusion.6, pred[24,8]{1,0:T(8,128)(4,1)S(1)} %iota_compare_fusion.3, bf16[24,8,64,64]{3,2,1,0:T(8,128)(2,1)} %bitcast.50, pred[24,8]{1,0:T(8,128)(4,1)S(1)} %compare_and_fusion.7, ...), kind=kOutput, calls=%fused_computation.13.clone.1 | convolution fusion | flops 103219200 | bytes 3932737 | tf_op jit(solution)/shard_map/while/body/eval_jaxpr/rpij,rpjl->ril/dot_general | solution.py:19
  71.1 0.8 compare_and_fusion.2
  72.0 0.1 reshape.102
  72.1 2.7 %gather_fusion.3 = bf16[192,64,64]{2,1,0:T(8,128)(2,1)} fusion(bf16[24,64,64]{2,1,0:T(8,128)(2,1)S(1)} %constant_dynamic-slice_fusion.4, s32[1024]{0:T(1024)S(1)} %pad_clamp_fusion.2), kind=kCustom, calls=%fused_computation.3.clone | custom fusion | bytes 3146496 | tf_op jit(solution)/shard_map/jit(_take)/gather | solution.py:15
  74.8 0.7 copy.25
  75.7 0.1 reshape.98
  75.8 2.7 %gather_fusion.2 = bf16[192,64,64]{2,1,0:T(8,128)(2,1)} fusion(bf16[24,64,64]{2,1,0:T(8,128)(2,1)S(1)} %get-tuple-element.207, s32[1024]{0:T(1024)S(1)} %pad_clamp_fusion.3), kind=kCustom, calls=%fused_computation.2.clone | custom fusion | bytes 3146496 | tf_op jit(solution)/shard_map/jit(_take)/gather | solution.py:14
  78.6 0.1 copy.23
  78.6 4.0 %fusion.29 = bf16[24,64,64]{2,1,0:T(8,128)(2,1)} fusion(f32[24,64,64]{2,1,0:T(8,128)} %get-tuple-element.206, bf16[24,8,64,64]{3,2,1,0:T(8,128)(2,1)S(1)} %bitcast.52, pred[24,8]{1,0:T(8,128)(4,1)} %copy.25, pred[24,8]{1,0:T(8,128)(4,1)S(1)} %iota_compare_fusion.1, bf16[24,8,64,64]{3,2,1,0:T(8,128)(2,1)} %bitcast.53, pred[24,8]{1,0:T(8,128)(4,1)S(1)} %copy.23), kind=kOutput, calls=%fused_computation.38 | convolution fusion | flops 103219200 | bytes 3736128 | tf_op jit(solution)/shard_map/rpij,rpjl->ril/dot_general | solution.py:19
  (53 shorter events, 1.3 us)
Async XLA Ops:
  0.0 1.8 %copy-start = (s32[48,4]{0,1:T(4,128)S(1)}, s32[48,4]{0,1:T(4,128)}, u32[]{:S(2)}) copy-start(s32[48,4]{0,1:T(4,128)} %param.11) | copy-start | bytes 2308
  31.5 15.2 %collective-permute-start = (bf16[24,64,64]{2,1,0:T(8,128)(2,1)S(1)}, bf16[24,64,64]{2,1,0:T(8,128)(2,1)S(1)}, u32[]{:S(2)}, u32[]{:S(2)}) collective-permute-start(bf16[24,64,64]{2,1,0:T(8,128)(2,1)S(1)} %copy.41), channel_id=1, source_target_pairs={{0,3},{1,0},{2,1},{3,2},{4,7},{5,4},{6,5},{7,6},{8,11},{9,8},{10,9... | collective-permute-start | bytes 589832 | tf_op jit(solution)/shard_map/while/body/eval_jaxpr/ppermute | solution.py:9
  46.7 12.7 %collective-permute-start = (bf16[24,64,64]{2,1,0:T(8,128)(2,1)S(1)}, bf16[24,64,64]{2,1,0:T(8,128)(2,1)S(1)}, u32[]{:S(2)}, u32[]{:S(2)}) collective-permute-start(bf16[24,64,64]{2,1,0:T(8,128)(2,1)S(1)} %copy.41), channel_id=1, source_target_pairs={{0,3},{1,0},{2,1},{3,2},{4,7},{5,4},{6,5},{7,6},{8,11},{9,8},{10,9... | collective-permute-start | bytes 589832 | tf_op jit(solution)/shard_map/while/body/eval_jaxpr/ppermute | solution.py:9
  59.5 11.6 %collective-permute-start = (bf16[24,64,64]{2,1,0:T(8,128)(2,1)S(1)}, bf16[24,64,64]{2,1,0:T(8,128)(2,1)S(1)}, u32[]{:S(2)}, u32[]{:S(2)}) collective-permute-start(bf16[24,64,64]{2,1,0:T(8,128)(2,1)S(1)} %copy.41), channel_id=1, source_target_pairs={{0,3},{1,0},{2,1},{3,2},{4,7},{5,4},{6,5},{7,6},{8,11},{9,8},{10,9... | collective-permute-start | bytes 589832 | tf_op jit(solution)/shard_map/while/body/eval_jaxpr/ppermute | solution.py:9
  75.8 2.8 %copy-start.1 = (bf16[192,64,64]{2,1,0:T(8,128)(2,1)S(1)}, bf16[192,64,64]{2,1,0:T(8,128)(2,1)}, u32[]{:S(2)}) copy-start(bf16[192,64,64]{2,1,0:T(8,128)(2,1)} %gather_fusion.3) | copy-start | bytes 4718596
where the time goes:
time: 83 us; the launch traced here: 82.6 us
  blocking collectives  29.6 us (36%)
  local copies, waits for them, and re-layouts  26.1 us (31%)
  matrix products  18.6 us (22%)
  starting transfers between devices  6.95 us (8%)
  other arithmetic  1.23 us (1%)
    all_gather x1, blocking collectives, on_device(): lax.all_gather(density_blocks, ('layer', 'row'), axis=0, tiled=True)  29.6 us
    dot_general x4, matrix products, block_terms(): jnp.einsum('rpij,rpjl->ril', picked_left, picked_right, preferred_element...  18.6 us
    gather x4, local copies, waits for them, and re-layouts, block_terms(): picked_left = jnp.take(left_panel, left_pick, axis=0)  10.9 us
    gather x4, local copies, waits for them, and re-layouts, block_terms(): picked_right = jnp.take(right_panel, right_pick, axis=0)  10.9 us
    ppermute x3, starting transfers between devices, passed_along(): lax.ppermute(shard, axis, [(i, (i + by) % devices) for i in range(devices)])  6.95 us
  transfers between devices with their start and end apart: 3, of which 0 were waited for; matrix products, arithmetic and copies ran while one was open for 39% of the time, Pallas kernels for 0%

commit v1 on v0

v1 whole, which is shorter than its diff:
```python
import functools

import jax
import jax.numpy as jnp
from jax import lax
from jax.experimental import pallas as pl
from jax.experimental.pallas import tpu as pltpu
from jax.sharding import PartitionSpec as P

MESH = pl.DeviceIdType.MESH


def kernel(
    cols, rows, layers, chunks,
    x_hbm, li_hbm, ri_hbm, cnt_hbm, out_ref,
    x_v, li_s, ri_s, cnt_s, lefts, rights, work_l, work_r, acc,
    in_sem, idx_sem, send_z, recv_z, send_x, recv_x,
):
    ns, blk, _ = x_hbm.shape
    half = ns // 2
    step_rows = half // chunks
    pairs = li_hbm.shape[2]
    c = lax.axis_index("col")
    layer = lax.axis_index("layer")
    row = lax.axis_index("row")
    r = layer * rows + row
    group = layers * rows

    own_rows = pl.ds(layer * ns, ns)
    x_copy = pltpu.make_async_copy(x_hbm, x_v, in_sem)
    x_copy.start()
    idx_copies = [
        pltpu.make_async_copy(src.at[own_rows], dst, idx_sem.at[j])
        for j, (src, dst) in enumerate(((li_hbm, li_s), (ri_hbm, ri_s), (cnt_hbm, cnt_s)))
    ]
    for copy in idx_copies:
        copy.start()

    barrier = pltpu.get_barrier_semaphore()

    @pl.when(c > 0)
    def _():
        pl.semaphore_signal(barrier, inc=1, device_id={"col": c - 1}, device_id_type=MESH)

    @pl.when(c < cols - 1)
    def _():
        pl.semaphore_signal(barrier, inc=1, device_id={"col": c + 1}, device_id_type=MESH)

    def mate(j):
        other = lax.rem(r + j, group)
        return other, {"layer": other // rows, "row": lax.rem(other, rows)}

    for j in range(1, group):
        pl.semaphore_signal(barrier, inc=1, device_id=mate(j)[1], device_id_type=MESH)

    x_copy.wait()
    for s in range(half):
        lefts[c, s] = jnp.concatenate([x_v[s], x_v[s + half]], axis=-1)
    near = jnp.where(c > 0, 1, 0) + jnp.where(c < cols - 1, 1, 0)
    pl.semaphore_wait(barrier, near + (group - 1))

    def z_copy(panel, chunk, way):
        part = lefts.at[panel, pl.ds(chunk * step_rows, step_rows)]
        return pltpu.make_async_remote_copy(
            src_ref=part,
            dst_ref=part,
            send_sem=send_z.at[way, panel, chunk],
            recv_sem=recv_z.at[panel, chunk],
            device_id={"col": c + (1 if way == 0 else -1)},
            device_id_type=MESH,
        )

    def x_copy_to(j):
        return pltpu.make_async_remote_copy(
            src_ref=lefts.at[c],
            dst_ref=rights.at[r],
            send_sem=send_x.at[j],
            recv_sem=recv_x.at[r],
            device_id=mate(j)[1],
            device_id_type=MESH,
        )

    def on_way(way, do):
        pl.when(c < cols - 1 if way == 0 else c > 0)(do)

    for chunk in range(chunks):
        for way in (0, 1):
            on_way(way, lambda chunk=chunk, way=way: z_copy(c, chunk, way).start())
        if chunk == 0:
            for j in range(1, group):
                x_copy_to(j).start()
    rights[r] = lefts[c]
    work_r[ns] = jnp.zeros_like(work_r[ns])
    acc[...] = jnp.zeros_like(acc)
    low = lax.broadcasted_iota(jnp.int32, (blk, 2 * blk), 1) < blk
    for copy in idx_copies:
        copy.wait()

    def multiply(k):
        @pl.when(k != r)
        def _():
            pltpu.make_async_remote_copy(
                src_ref=lefts.at[c],
                dst_ref=rights.at[k],
                send_sem=send_x.at[0],
                recv_sem=recv_x.at[k],
                device_id=mate(1)[1],
                device_id_type=MESH,
            ).wait_recv()

        for s in range(half):
            block = lefts[k, s]
            turned = jnp.concatenate([block[:, blk:], block[:, :blk]], axis=-1)
            work_l[s] = block
            work_l[s + half] = turned
            work_l[s + 2 * half] = block
            block = rights[k, s]
            work_r[s] = block
            work_r[s + half] = jnp.concatenate([block[:, blk:], block[:, :blk]], axis=-1)

        def one(o, carry):
            count = cnt_s[o, k]
            left, right = [], []
            for p in range(0, pairs, 2):
                first = work_l[li_s[o, k, p]]
                second = work_l[li_s[o, k, p + 1] + half]
                left.append(jnp.where(low, first, second))
                for q in (p, p + 1):
                    right.append(work_r[jnp.where(q < count, ri_s[o, k, q], ns)])
            acc[o] += jnp.dot(
                jnp.concatenate(left, axis=1),
                jnp.concatenate(right, axis=0),
                preferred_element_type=jnp.float32,
            )
            return carry

        lax.fori_loop(0, ns, one, 0, unroll=2)

    multiply(c)

    def step(s, carry):
        from_low = c - 1 - s
        from_high = c + 1 + s
        for chunk in range(chunks):

            @pl.when(from_low >= 0)
            def _(chunk=chunk):
                z_copy(from_low, chunk, 0).wait_recv()

                @pl.when(c < cols - 1)
                def _():
                    z_copy(from_low, chunk, 0).start()

            @pl.when(from_high < cols)
            def _(chunk=chunk):
                z_copy(from_high, chunk, 1).wait_recv()

                @pl.when(c > 0)
                def _():
                    z_copy(from_high, chunk, 1).start()

        @pl.when(from_low >= 0)
        def _():
            multiply(from_low)

        @pl.when(from_high < cols)
        def _():
            multiply(from_high)

        return carry

    lax.fori_loop(0, cols - 1, step, 0)

    for o in range(ns):
        out_ref[o] = acc[o][:, :blk].astype(out_ref.dtype)

    def drain(panel, carry):
        for chunk in range(chunks):

            @pl.when((c < cols - 1) & (panel <= c))
            def _(chunk=chunk):
                z_copy(panel, chunk, 0).wait_send()

            @pl.when((c > 0) & (panel >= c))
            def _(chunk=chunk):
                z_copy(panel, chunk, 1).wait_send()

        return carry

    lax.fori_loop(0, cols, drain, 0)
    for j in range(1, group):
        x_copy_to(j).wait_send()


def on_device(density_blocks, left_index, right_index, pair_count):
    ns, blk, _ = density_blocks.shape
    cols = lax.axis_size("col")
    rows = lax.axis_size("row")
    layers = lax.axis_size("layer")
    inner = left_index.shape[1]
    pairs = left_index.shape[2]
    half = ns // 2
    chunks = 2 if half % 2 == 0 else 1
    group = rows * layers
    packed = (half, blk, 2 * blk)
    return pl.pallas_call(
        functools.partial(kernel, cols, rows, layers, chunks),
        out_shape=jax.ShapeDtypeStruct((ns, blk, blk), jnp.bfloat16),
        in_specs=[pl.BlockSpec(memory_space=pl.ANY)] * 4,
        out_specs=pl.BlockSpec(memory_space=pltpu.VMEM),
        scratch_shapes=[
            pltpu.VMEM((ns, blk, blk), jnp.bfloat16),
            pltpu.SMEM((ns, inner, pairs), jnp.int32),
            pltpu.SMEM((ns, inner, pairs), jnp.int32),
            pltpu.SMEM((ns, inner), jnp.int32),
            pltpu.VMEM((cols,) + packed, jnp.bfloat16),
            pltpu.VMEM((group,) + packed, jnp.bfloat16),
            pltpu.VMEM((3 * half, blk, 2 * blk), jnp.bfloat16),
            pltpu.VMEM((ns + 1, blk, 2 * blk), jnp.bfloat16),
            pltpu.VMEM((ns, blk, 2 * blk), jnp.float32),
            pltpu.SemaphoreType.DMA,
            pltpu.SemaphoreType.DMA((3,)),
            pltpu.SemaphoreType.DMA((2, cols, chunks)),
            pltpu.SemaphoreType.DMA((cols, chunks)),
            pltpu.SemaphoreType.DMA((group,)),
            pltpu.SemaphoreType.DMA((group,)),
        ],
        compiler_params=pltpu.CompilerParams(
            collective_id=0, has_side_effects=True, vmem_limit_bytes=32 * 1024 * 1024
        ),
    )(density_blocks, left_index, right_index, pair_count)


def solution(mesh):
    placed = (
        P(("parts", "layer", "row"), "col", None),
        P(("parts", "row"), "col", None),
        P(("parts", "row"), "col", None),
        P(("parts", "row"), "col"),
    )
    return jax.shard_map(
        on_device,
        mesh=mesh,
        in_specs=placed,
        out_specs=P(("parts", "layer", "row"), "col", None),
        check_vma=False,
    )
```

time: 83 us -> 32.8 us (0.40)
  blocking collectives: 29.6 us -> 0 us
  Pallas kernels: 0 us -> 29.2 us
  local copies, waits for them, and re-layouts: 26.1 us -> 3.33 us
  matrix products: 18.6 us -> 0 us
  starting transfers between devices: 6.95 us -> 0 us
  other arithmetic: 1.23 us -> 0 us
    all_gather x1 -> x0, blocking collectives: 29.6 us -> none  [on_device(): lax.all_gather(density_blocks, ('layer', 'row'), axis=0, tiled=True)]
    pallas_call x0 -> x1, Pallas kernels: none -> 29.2 us  [on_device(): pl.pallas_call(functools.partial(kernel, cols, rows, layers, chunks), out...]
    gather x8 -> x0, local copies, waits for them, and re-layouts: 21.8 us -> none  [the longest x4 10.9 us: block_terms(): picked_left = jnp.take(left_panel, left_pick, axis=0)]
    dot_general x4 -> x0, matrix products: 18.6 us -> none  [block_terms(): jnp.einsum('rpij,rpjl->ril', picked_left, picked_right, preferred_element...]
    ppermute x3 -> x0, starting transfers between devices: 6.95 us -> none  [passed_along(): lax.ppermute(shard, axis, [(i, (i + by) % devices) for i in range(devices)])]
    unnamed x5 -> x10, local copies, waits for them, and re-layouts: 1.02 us -> 3.33 us
    dynamic_slice x19 -> x0, local copies, waits for them, and re-layouts: 1.55 us -> none  [the longest x1 0.81 us: on_device(): lax.dynamic_slice_in_dim(right_index, layer_at * slot_count, slot_count, 0)]
    and x7 -> x0, other arithmetic: 0.84 us -> none  [the longest x4 0.81 us: block_terms(): picked_right = jnp.take(right_panel, right_pick, axis=0)]
  transfers between devices with their start and end apart: 3 -> 0, of which waited for: 0 -> 0; matrix products, arithmetic and copies ran while one was open for 39% -> 0% of each run, Pallas kernels for 0% -> 0%
where the time goes in v1:
time: 32.8 us; the launch traced here: 32.5 us
  Pallas kernels  29.2 us (89%)
  local copies, waits for them, and re-layouts  3.33 us (10%)
    pallas_call x1, Pallas kernels, on_device(): pl.pallas_call(functools.partial(kernel, cols, rows, layers, chunks), out...  29.2 us
    unnamed x10, local copies, waits for them, and re-layouts  3.33 us

profile of v1, /device:TPU:0, one launch (start us, length us, event | category | flops | bytes accessed | tf_op | source)
XLA Modules:
  0.0 32.5 jit_solution(7344050460053578834)
XLA Ops:
  0.0 0.0 copy-start.1
  0.0 0.8 %copy.7.cnt_hbm = s32[48,4]{1,0:T(8,128)S(1)} copy(s32[48,4]{0,1:T(4,128)} %param.7) | data formatting | bytes 1536 | tf_op args[3]
  0.8 0.0 copy-done.1
  0.8 0.0 copy-start.2
  0.8 0.1 copy.5.li_hbm
  0.9 0.6 %copy-done.2 = s32[48,4,8]{0,2,1:T(8,128)S(1)} copy-done((s32[48,4,8]{0,2,1:T(8,128)S(1)}, s32[48,4,8]{0,2,1:T(8,128)}, u32[]{:S(2)}) %copy-start.2) | copy-done | bytes 6168
  1.5 0.1 copy.6.ri_hbm
  1.6 0.0 copy-start
  1.6 1.0 %copy-done = bf16[24,64,64]{2,1,0:T(8,128)(2,1)S(1)} copy-done((bf16[24,64,64]{2,1,0:T(8,128)(2,1)S(1)}, bf16[24,64,64]{2,1,0:T(8,128)(2,1)}, u32[]{:S(2)}) %copy-start) | copy-done | bytes 196632
  2.6 29.2 %shard_map.46 = bf16[24,64,64]{2,1,0:T(8,128)(2,1)S(1)} custom-call(bf16[24,64,64]{2,1,0:T(8,128)(2,1)S(1)} %copy-done, s32[48,4,8]{2,1,0:T(4,128)S(1)} %copy.5.li_hbm, s32[48,4,8]{2,1,0:T(4,128)S(1)} %copy.6.ri_hbm, s32[48,4]{1,0:T(8,128)S(1)} %copy.7.cnt_hbm), custom_call_target="tpu_custom_call" | custom-call | tf_op jit(solution)/shard_map/pallas_call | solution.py:206
  31.8 0.7 %copy.9 = bf16[24,64,64]{2,1,0:T(8,128)(2,1)} copy(bf16[24,64,64]{2,1,0:T(8,128)(2,1)S(1)} %shard_map.46) | data formatting | bytes 393216
Async XLA Ops:
  0.0 0.8 %copy-start.1 = (s32[48,4,8]{0,2,1:T(8,128)S(1)}, s32[48,4,8]{0,2,1:T(8,128)}, u32[]{:S(2)}) copy-start(s32[48,4,8]{0,2,1:T(8,128)} %param.5) | copy-start | bytes 18436
  0.8 0.7 %copy-start.2 = (s32[48,4,8]{0,2,1:T(8,128)S(1)}, s32[48,4,8]{0,2,1:T(8,128)}, u32[]{:S(2)}) copy-start(s32[48,4,8]{0,2,1:T(8,128)} %param.6) | copy-start | bytes 18436
  1.6 1.0 %copy-start = (bf16[24,64,64]{2,1,0:T(8,128)(2,1)S(1)}, bf16[24,64,64]{2,1,0:T(8,128)(2,1)}, u32[]{:S(2)}) copy-start(bf16[24,64,64]{2,1,0:T(8,128)(2,1)} %x_hbm.1) | copy-start | bytes 589828

commit v2 on v1

v2 whole, which is shorter than its diff:
```python
import functools

import jax
import jax.numpy as jnp
from jax import lax
from jax.experimental import pallas as pl
from jax.experimental.pallas import tpu as pltpu
from jax.sharding import PartitionSpec as P

UNROLL = 24
MESH = pl.DeviceIdType.MESH


def kernel(
    cols, rows, layers, chunks,
    x_hbm, li_hbm, ri_hbm, cnt_hbm, out_ref,
    x_v, li_s, ri_s, cnt_s, lefts, rights, work_l, work_r, acc,
    in_sem, idx_sem, send_z, recv_z, send_x, send_l, recv_x,
):
    ns, blk, _ = x_hbm.shape
    half = ns // 2
    step_rows = half // chunks
    pairs = li_hbm.shape[1]
    c = lax.axis_index("col")
    layer = lax.axis_index("layer")
    row = lax.axis_index("row")
    r = layer * rows + row

    x_copy = pltpu.make_async_copy(x_hbm, x_v, in_sem)
    x_copy.start()
    idx_copies = [
        pltpu.make_async_copy(src, dst, idx_sem.at[j])
        for j, (src, dst) in enumerate(((li_hbm, li_s), (ri_hbm, ri_s), (cnt_hbm, cnt_s)))
    ]
    for copy in idx_copies:
        copy.start()

    barrier = pltpu.get_barrier_semaphore()

    @pl.when(c > 0)
    def _():
        pl.semaphore_signal(barrier, inc=1, device_id={"col": c - 1}, device_id_type=MESH)

    @pl.when(c < cols - 1)
    def _():
        pl.semaphore_signal(barrier, inc=1, device_id={"col": c + 1}, device_id_type=MESH)

    def row_mate(j):
        other = lax.rem(row + j, rows)
        return other, {"row": other}

    def layer_mate(j):
        other = lax.rem(layer + j, layers)
        return other, {"layer": other}

    for j in range(1, rows):
        pl.semaphore_signal(barrier, inc=1, device_id=row_mate(j)[1], device_id_type=MESH)
    for j in range(1, layers):
        pl.semaphore_signal(barrier, inc=1, device_id=layer_mate(j)[1], device_id_type=MESH)

    x_copy.wait()
    for s in range(half):
        both = jnp.concatenate([x_v[s], x_v[s + half]], axis=-1)
        lefts[c, s] = both
        rights[r, s] = both
    near = jnp.where(c > 0, 1, 0) + jnp.where(c < cols - 1, 1, 0)
    pl.semaphore_wait(barrier, near + (rows - 1) + (layers - 1))

    def z_copy(panel, chunk, way):
        part = lefts.at[panel, pl.ds(chunk * step_rows, step_rows)]
        return pltpu.make_async_remote_copy(
            src_ref=part,
            dst_ref=part,
            send_sem=send_z.at[way, panel, chunk],
            recv_sem=recv_z.at[panel, chunk],
            device_id={"col": c + (1 if way == 0 else -1)},
            device_id_type=MESH,
        )

    def row_copy(j):
        return pltpu.make_async_remote_copy(
            src_ref=lefts.at[c],
            dst_ref=rights.at[r],
            send_sem=send_x.at[j],
            recv_sem=recv_x.at[r],
            device_id=row_mate(j)[1],
            device_id_type=MESH,
        )

    def layer_copy(j, other):
        panel = layer * rows + other
        return pltpu.make_async_remote_copy(
            src_ref=rights.at[panel],
            dst_ref=rights.at[panel],
            send_sem=send_l.at[j, other],
            recv_sem=recv_x.at[panel],
            device_id=layer_mate(j)[1],
            device_id_type=MESH,
        )

    def right_landed(panel):
        pltpu.make_async_remote_copy(
            src_ref=rights.at[panel],
            dst_ref=rights.at[panel],
            send_sem=send_x.at[0],
            recv_sem=recv_x.at[panel],
            device_id=row_mate(1)[1],
            device_id_type=MESH,
        ).wait_recv()

    def on_way(way, do):
        pl.when(c < cols - 1 if way == 0 else c > 0)(do)

    for chunk in range(chunks):
        for way in (0, 1):
            on_way(way, lambda chunk=chunk, way=way: z_copy(c, chunk, way).start())
        if chunk == 0:
            for j in range(1, rows):
                row_copy(j).start()
            for j in range(1, layers):
                layer_copy(j, row).start()
    work_r[ns] = jnp.zeros_like(work_r[ns])
    acc[...] = jnp.zeros_like(acc)
    low = lax.broadcasted_iota(jnp.int32, (blk, 2 * blk), 1) < blk
    for copy in idx_copies:
        copy.wait()

    def multiply(k):
        @pl.when(k // rows != layer)
        def _():
            right_landed(k)

        for s in range(half):
            block = lefts[k, s]
            turned = jnp.concatenate([block[:, blk:], block[:, :blk]], axis=-1)
            work_l[s] = block
            work_l[s + half] = turned
            work_l[s + 2 * half] = block
            block = rights[k, s]
            work_r[s] = block
            work_r[s + half] = jnp.concatenate([block[:, blk:], block[:, :blk]], axis=-1)

        def one(o, carry):
            at = layer * ns + o
            count = cnt_s[k, at]
            left, right = [], []
            for p in range(0, pairs, 2):
                first = work_l[li_s[k, p, at]]
                second = work_l[li_s[k, p + 1, at] + half]
                left.append(jnp.where(low, first, second))
                for q in (p, p + 1):
                    right.append(work_r[jnp.where(q < count, ri_s[k, q, at], ns)])
            acc[o] += jnp.dot(
                jnp.concatenate(left, axis=1),
                jnp.concatenate(right, axis=0),
                preferred_element_type=jnp.float32,
            )
            return carry

        lax.fori_loop(0, ns, one, 0, unroll=UNROLL)

    shorter = jnp.minimum(c, cols - 1 - c)
    longer = jnp.maximum(c, cols - 1 - c)

    def turn(i):
        both = i <= 2 * shorter
        distance = jnp.where(both, (i + 1) // 2, i - shorter)
        lower = jnp.where(both, lax.rem(i, 2) == 1, c == longer)
        return jnp.where(lower, c - distance, c + distance)

    def landed(distance):
        return 1 + jnp.minimum(c, distance) + jnp.minimum(cols - 1 - c, distance)

    def multiply_turn(i, carry):
        multiply(turn(i))
        return carry

    def step(s, done):
        from_low = c - 1 - s
        from_high = c + 1 + s
        for chunk in range(chunks):

            @pl.when(from_low >= 0)
            def _(chunk=chunk):
                z_copy(from_low, chunk, 0).wait_recv()

                @pl.when(c < cols - 1)
                def _():
                    z_copy(from_low, chunk, 0).start()

            @pl.when(from_high < cols)
            def _(chunk=chunk):
                z_copy(from_high, chunk, 1).wait_recv()

                @pl.when(c > 0)
                def _():
                    z_copy(from_high, chunk, 1).start()

        @pl.when(s == 0)
        def _():
            for j in range(1, rows):
                other = row_mate(j)[0]
                right_landed(layer * rows + other)
                for to in range(1, layers):
                    layer_copy(to, other).start()

        eager = (shorter == 0) | (s + 1 >= longer)
        until = jnp.where(eager, landed(s + 1), landed(s))
        lax.fori_loop(done, until, multiply_turn, 0)
        return until

    lax.fori_loop(0, cols - 1, step, 0)

    for o in range(ns):
        out_ref[o] = acc[o][:, :blk].astype(out_ref.dtype)

    def drain(panel, carry):
        for chunk in range(chunks):

            @pl.when((c < cols - 1) & (panel <= c))
            def _(chunk=chunk):
                z_copy(panel, chunk, 0).wait_send()

            @pl.when((c > 0) & (panel >= c))
            def _(chunk=chunk):
                z_copy(panel, chunk, 1).wait_send()

        return carry

    lax.fori_loop(0, cols, drain, 0)
    for j in range(1, rows):
        row_copy(j).wait_send()
    for j in range(1, layers):
        for other in range(rows):
            layer_copy(j, other).wait_send()


def on_device(density_blocks, left_index, right_index, pair_count):
    ns, blk, _ = density_blocks.shape
    cols = lax.axis_size("col")
    rows = lax.axis_size("row")
    layers = lax.axis_size("layer")
    left_index = jnp.transpose(left_index, (1, 2, 0))
    right_index = jnp.transpose(right_index, (1, 2, 0))
    pair_count = jnp.transpose(pair_count, (1, 0))
    half = ns // 2
    chunks = 3 if half % 3 == 0 else 1
    group = rows * layers
    packed = (half, blk, 2 * blk)
    return pl.pallas_call(
        functools.partial(kernel, cols, rows, layers, chunks),
        out_shape=jax.ShapeDtypeStruct((ns, blk, blk), jnp.bfloat16),
        in_specs=[pl.BlockSpec(memory_space=pltpu.HBM)] * 4,
        out_specs=pl.BlockSpec(memory_space=pltpu.VMEM),
        scratch_shapes=[
            pltpu.VMEM((ns, blk, blk), jnp.bfloat16),
            pltpu.SMEM(left_index.shape, jnp.int32),
            pltpu.SMEM(right_index.shape, jnp.int32),
            pltpu.SMEM(pair_count.shape, jnp.int32),
            pltpu.VMEM((cols,) + packed, jnp.bfloat16),
            pltpu.VMEM((group,) + packed, jnp.bfloat16),
            pltpu.VMEM((3 * half, blk, 2 * blk), jnp.bfloat16),
            pltpu.VMEM((ns + 1, blk, 2 * blk), jnp.bfloat16),
            pltpu.VMEM((ns, blk, 2 * blk), jnp.float32),
            pltpu.SemaphoreType.DMA,
            pltpu.SemaphoreType.DMA((3,)),
            pltpu.SemaphoreType.DMA((2, cols, chunks)),
            pltpu.SemaphoreType.DMA((cols, chunks)),
            pltpu.SemaphoreType.DMA((rows,)),
            pltpu.SemaphoreType.DMA((layers, rows)),
            pltpu.SemaphoreType.DMA((group,)),
        ],
        compiler_params=pltpu.CompilerParams(
            collective_id=0, has_side_effects=True, vmem_limit_bytes=60 * 1024 * 1024
        ),
    )(density_blocks, left_index, right_index, pair_count)


def solution(mesh):
    placed = (
        P(("parts", "layer", "row"), "col", None),
        P(("parts", "row"), "col", None),
        P(("parts", "row"), "col", None),
        P(("parts", "row"), "col"),
    )
    return jax.shard_map(
        on_device,
        mesh=mesh,
        in_specs=placed,
        out_specs=P(("parts", "layer", "row"), "col", None),
        check_vma=False,
    )
```

time: 32.8 us -> 23.6 us (0.72)
  Pallas kernels: 29.2 us -> 21.7 us
  local copies, waits for them, and re-layouts: 3.33 us -> 1.77 us
    pallas_call x1, Pallas kernels: 29.2 us -> 21.7 us  [on_device(): pl.pallas_call(functools.partial(kernel, cols, rows, layers, chunks), out...]
    unnamed x10 -> x1, local copies, waits for them, and re-layouts: 3.33 us -> 1.77 us
where the time goes in v2:
time: 23.6 us; the launch traced here: 23.5 us
  Pallas kernels  21.7 us (92%)
  local copies, waits for them, and re-layouts  1.77 us (7%)
    pallas_call x1, Pallas kernels, on_device(): pl.pallas_call(functools.partial(kernel, cols, rows, layers, chunks), out...  21.7 us
    unnamed x1, local copies, waits for them, and re-layouts  1.77 us

profile of v2, /device:TPU:0, one launch (start us, length us, event | category | flops | bytes accessed | tf_op | source)
XLA Modules:
  0.0 23.5 jit_solution(2133203278081592378)
XLA Ops:
  0.0 21.7 %shard_map.46 = bf16[24,64,64]{2,1,0:T(8,128)(2,1)} custom-call(bf16[24,64,64]{2,1,0:T(8,128)(2,1)} %x_hbm.1, s32[4,8,48]{2,1,0:T(8,128)} %bitcast.3, s32[4,8,48]{2,1,0:T(8,128)} %bitcast.4, s32[4,48]{1,0:T(4,128)} %bitcast.5), custom_call_target="tpu_custom_call" | custom-call | tf_op jit(solution)/shard_map/pallas_call | solution.py:250
  21.7 1.8 %copy.6 = bf16[24,64,64]{2,1,0:T(8,128)(2,1)} copy(bf16[24,64,64]{2,1,0:T(8,128)(2,1)} %shard_map.46) | data formatting | bytes 393216

commit v3 on v2

--- a/solution.py
+++ b/solution.py
@@ -244,7 +244,7 @@
     right_index = jnp.transpose(right_index, (1, 2, 0))
     pair_count = jnp.transpose(pair_count, (1, 0))
     half = ns // 2
-    chunks = 3 if half % 3 == 0 else 1
+    chunks = 2 if half % 2 == 0 else 1
     group = rows * layers
     packed = (half, blk, 2 * blk)
     return pl.pallas_call(

time: 23.6 us -> 23.4 us (level)
  Pallas kernels: 21.7 us -> 21.4 us
    pallas_call x1, Pallas kernels: 21.7 us -> 21.4 us  [on_device(): pl.pallas_call(functools.partial(kernel, cols, rows, layers, chunks), out...]
where the time goes in v3:
time: 23.4 us; the launch traced here: 23.2 us
  Pallas kernels  21.4 us (91%)
  local copies, waits for them, and re-layouts  1.77 us (8%)
    pallas_call x1, Pallas kernels, on_device(): pl.pallas_call(functools.partial(kernel, cols, rows, layers, chunks), out...  21.4 us
    unnamed x1, local copies, waits for them, and re-layouts  1.77 us

profile of v3, /device:TPU:0, one launch (start us, length us, event | category | flops | bytes accessed | tf_op | source)
XLA Modules:
  0.0 23.2 jit_solution(2595187307174735114)
XLA Ops:
  0.0 21.4 %shard_map.46 = bf16[24,64,64]{2,1,0:T(8,128)(2,1)} custom-call(bf16[24,64,64]{2,1,0:T(8,128)(2,1)} %x_hbm.1, s32[4,8,48]{2,1,0:T(8,128)} %bitcast.3, s32[4,8,48]{2,1,0:T(8,128)} %bitcast.4, s32[4,48]{1,0:T(4,128)} %bitcast.5), custom_call_target="tpu_custom_call" | custom-call | tf_op jit(solution)/shard_map/pallas_call | solution.py:250
  21.4 1.8 %copy.6 = bf16[24,64,64]{2,1,0:T(8,128)(2,1)} copy(bf16[24,64,64]{2,1,0:T(8,128)(2,1)} %shard_map.46) | data formatting | bytes 393216

commit v4 on v3

--- a/solution.py
+++ b/solution.py
@@ -26,8 +26,13 @@
     row = lax.axis_index("row")
     r = layer * rows + row
 
-    x_copy = pltpu.make_async_copy(x_hbm, x_v, in_sem)
-    x_copy.start()
+    def x_copy(chunk, side):
+        part = pl.ds(side * half + chunk * step_rows, step_rows)
+        return pltpu.make_async_copy(x_hbm.at[part], x_v.at[part], in_sem.at[chunk, side])
+
+    for chunk in range(chunks):
+        for side in (0, 1):
+            x_copy(chunk, side).start()
     idx_copies = [
         pltpu.make_async_copy(src, dst, idx_sem.at[j])
         for j, (src, dst) in enumerate(((li_hbm, li_s), (ri_hbm, ri_s), (cnt_hbm, cnt_s)))
@@ -58,11 +63,6 @@
     for j in range(1, layers):
         pl.semaphore_signal(barrier, inc=1, device_id=layer_mate(j)[1], device_id_type=MESH)
 
-    x_copy.wait()
-    for s in range(half):
-        both = jnp.concatenate([x_v[s], x_v[s + half]], axis=-1)
-        lefts[c, s] = both
-        rights[r, s] = both
     near = jnp.where(c > 0, 1, 0) + jnp.where(c < cols - 1, 1, 0)
     pl.semaphore_wait(barrier, near + (rows - 1) + (layers - 1))
 
@@ -112,13 +112,18 @@
         pl.when(c < cols - 1 if way == 0 else c > 0)(do)
 
     for chunk in range(chunks):
+        for side in (0, 1):
+            x_copy(chunk, side).wait()
+        for t in range(chunk * step_rows, (chunk + 1) * step_rows):
+            both = jnp.concatenate([x_v[t], x_v[t + half]], axis=-1)
+            lefts[c, t] = both
+            rights[r, t] = both
         for way in (0, 1):
             on_way(way, lambda chunk=chunk, way=way: z_copy(c, chunk, way).start())
-        if chunk == 0:
-            for j in range(1, rows):
-                row_copy(j).start()
-            for j in range(1, layers):
-                layer_copy(j, row).start()
+    for j in range(1, rows):
+        row_copy(j).start()
+    for j in range(1, layers):
+        layer_copy(j, row).start()
     work_r[ns] = jnp.zeros_like(work_r[ns])
     acc[...] = jnp.zeros_like(acc)
     low = lax.broadcasted_iota(jnp.int32, (blk, 2 * blk), 1) < blk
@@ -262,7 +267,7 @@
             pltpu.VMEM((3 * half, blk, 2 * blk), jnp.bfloat16),
             pltpu.VMEM((ns + 1, blk, 2 * blk), jnp.bfloat16),
             pltpu.VMEM((ns, blk, 2 * blk), jnp.float32),
-            pltpu.SemaphoreType.DMA,
+            pltpu.SemaphoreType.DMA((chunks, 2)),
             pltpu.SemaphoreType.DMA((3,)),
             pltpu.SemaphoreType.DMA((2, cols, chunks)),
             pltpu.SemaphoreType.DMA((cols, chunks)),

time: 23.4 us -> 23.5 us (level)
  no operation moved by 1% of the time
where the time goes in v4:
time: 23.5 us; the launch traced here: 23.3 us
  Pallas kernels  21.6 us (92%)
  local copies, waits for them, and re-layouts  1.77 us (8%)
    pallas_call x1, Pallas kernels, on_device(): pl.pallas_call(functools.partial(kernel, cols, rows, layers, chunks), out...  21.6 us
    unnamed x1, local copies, waits for them, and re-layouts  1.77 us

profile of v4, /device:TPU:0, one launch (start us, length us, event | category | flops | bytes accessed | tf_op | source)
XLA Modules:
  0.0 23.3 jit_solution(660175175459216430)
XLA Ops:
  0.0 21.6 %shard_map.46 = bf16[24,64,64]{2,1,0:T(8,128)(2,1)} custom-call(bf16[24,64,64]{2,1,0:T(8,128)(2,1)} %x_hbm.1, s32[4,8,48]{2,1,0:T(8,128)} %bitcast.3, s32[4,8,48]{2,1,0:T(8,128)} %bitcast.4, s32[4,48]{1,0:T(4,128)} %bitcast.5), custom_call_target="tpu_custom_call" | custom-call | tf_op jit(solution)/shard_map/pallas_call | solution.py:255
  21.6 1.8 %copy.6 = bf16[24,64,64]{2,1,0:T(8,128)(2,1)} copy(bf16[24,64,64]{2,1,0:T(8,128)(2,1)} %shard_map.46) | data formatting | bytes 393216
